TPU v7x, 32 devices: a whole 2x2x4 slice. The times are simulated.
32 devices in a mesh: groups: 2 (over y), lon: 4 (over z), lat: 2 (over x), sub: 2 (over core).
Axes of the slice: x: 2, y: 2, z: 4, core: 2. Of those that a mesh axis runs over, the one named last changes fastest.
Arguments:
- grid_latent: bfloat16 [32768, 256], P(('groups', 'lon', 'lat', 'sub')), parts along dimension 0, may hold values from -6 to 6
- mesh_latent: float32 [32, 512, 256], P(('groups', 'lat'), ('lon', 'sub')), parts along dimension 0, may hold values from -6 to 6
- block_owner: int32 [128, 1], P(('lon', 'lat', 'sub')), may hold values from 0 to 7; in each aligned block of 8 rows (0 to 7, 8 to 15, ...) at most 2 rows name the same one
- block_sender: int32 [128, 128], P(('lon', 'lat', 'sub')), may hold values from 0 to 1023
- block_receiver: int32 [128, 128], P(('lon', 'lat', 'sub')), may hold values from 0 to 512, as said below
- block_feature: bfloat16 [128, 4, 128], P(('lon', 'lat', 'sub')), may hold values from -6 to 6
- mesh_sender: int32 [256, 128], P(('lon', 'lat', 'sub')), may hold values from 0 to 815, as said below
- mesh_receiver: int32 [256, 128], P(('lon', 'lat', 'sub')), may hold values from 0 to 511
- mesh_feature: bfloat16 [256, 4, 128], P(('lon', 'lat', 'sub')), may hold values from -6 to 6
- encoder_edge_input: bfloat16 [512, 256], replicated, may hold values from -0.25 to 0.25
- encoder_edge_feature: float32 [4, 256], replicated, may hold values from -3 to 3
- encoder_edge_bias: float32 [256], replicated, may hold values from -3 to 3
- encoder_edge_output: bfloat16 [256, 256], replicated, may hold values from -0.375 to 0.375
- encoder_edge_gain: float32 [256], replicated, may hold values from 0.5 to 1.5
- encoder_node_input: bfloat16 [512, 256], replicated, may hold values from -0.25 to 0.25
- encoder_node_bias: float32 [256], replicated, may hold values from -3 to 3
- encoder_node_output: bfloat16 [256, 256], replicated, may hold values from -0.375 to 0.375
- encoder_node_gain: float32 [256], replicated, may hold values from 0.5 to 1.5
- processor_edge_input: bfloat16 [512, 256], replicated, may hold values from -0.25 to 0.25
- processor_edge_feature: float32 [4, 256], replicated, may hold values from -3 to 3
- processor_edge_bias: float32 [256], replicated, may hold values from -3 to 3
- processor_edge_output: bfloat16 [256, 256], replicated, may hold values from -0.375 to 0.375
- processor_edge_gain: float32 [256], replicated, may hold values from 0.5 to 1.5
- processor_node_input: bfloat16 [512, 256], replicated, may hold values from -0.25 to 0.25
- processor_node_bias: float32 [256], replicated, may hold values from -3 to 3
- processor_node_output: bfloat16 [256, 256], replicated, may hold values from -0.375 to 0.375
- processor_node_gain: float32 [256], replicated, may hold values from 0.5 to 1.5
Outputs:
- mesh_out: float32 [32, 512, 256], P(('groups', 'lat'), ('lon', 'sub')), parts along dimension 0
There are 2 independent parts, one for each index of `groups`. A program takes and returns all parts, laid end to end along the dimension named above; an argument that names none is the same for every part. Nothing has to cross between parts.
Inputs may be any that keep to these rules, and one draw needn't show every extreme that they name: `block_owner`: among the 8 blocks of one device no owner is named more than 2 times, a bound that some block reaches. `block_receiver`: each block ends with 1 to 32 padding rows holding 512. `mesh_sender`: A sender cell lies at most 2 rows and 2 columns away from its receiver's cell in the extended block, whose node (a, b) is cell (a + 2) * 68 + b + 2. The first row of each device's first block joins its last node with the last cell, the second row its first node with cell 0.
All inputs are finite; a program needn't handle non-finite values.
Results may differ from a plain program's by a relative error of at most 0.0043.
Values may be sent and summed in bfloat16 or wider, within the bound.
A program may use at most 64 MiB of HBM per device.

v0:
```python
import math

import jax
import jax.numpy as jnp
from jax import lax
from jax.sharding import PartitionSpec as P

CAP = 2
W = 2


def with_halo(array, sides, width, wrap):
    for axis, dim in sides:
        size, length = (lax.axis_size(axis), array.shape[dim])
        up = [(i, (i + 1) % size) for i in range(size if wrap else size - 1)]
        down = [(j, i) for i, j in up]
        last = lax.slice_in_dim(array, length - width, length, axis=dim)
        first = lax.slice_in_dim(array, 0, width, axis=dim)
        before = lax.ppermute(last, axis, up)
        after = lax.ppermute(first, axis, down)
        array = jnp.concatenate([before, array, after], axis=dim)
    return array


def layer_norm(values, norm_gain):
    center = values - jnp.mean(values, axis=-1, keepdims=True)
    spread = jnp.mean(center * center, axis=-1, keepdims=True)
    return center * lax.rsqrt(spread + 1e-05) * norm_gain


def edge_update(
    senders, receivers, features, input_weight, feature_weight, offset, output_weight, norm_gain
):
    channels = senders.shape[-1]
    preact = jnp.dot(senders, input_weight[:channels], preferred_element_type=jnp.float32)
    preact = preact + jnp.dot(
        receivers, input_weight[channels:], preferred_element_type=jnp.float32
    )
    preact = (
        preact
        + jnp.dot(features.astype(jnp.float32), feature_weight, precision=lax.Precision.HIGHEST)
        + offset
    )
    hidden = jax.nn.silu(preact).astype(jnp.bfloat16)
    projected = jnp.dot(hidden, output_weight, preferred_element_type=jnp.float32)
    return layer_norm(projected, norm_gain).astype(jnp.bfloat16)


def node_update(mesh_rows, mesh_bf, summed, input_weight, offset, output_weight, norm_gain):
    channels = mesh_rows.shape[-1]
    preact = jnp.dot(mesh_bf, input_weight[:channels], preferred_element_type=jnp.float32)
    preact = (
        preact
        + jnp.dot(
            summed.astype(jnp.bfloat16), input_weight[channels:], preferred_element_type=jnp.float32
        )
        + offset
    )
    hidden = jax.nn.silu(preact).astype(jnp.bfloat16)
    projected = jnp.dot(hidden, output_weight, preferred_element_type=jnp.float32)
    return mesh_rows + layer_norm(projected, norm_gain)


def pick_rows(table, row_ids):
    flat_ids = row_ids.reshape(-1).astype(jnp.int32)
    total = flat_ids.shape[0]
    span = math.gcd(total, 1024)
    table_rows = jnp.arange(table.shape[0], dtype=jnp.int32)

    def one_block(block_ids):
        selector = (block_ids[:, None] == table_rows[None, :]).astype(jnp.bfloat16)
        return jnp.dot(selector, table, preferred_element_type=jnp.float32).astype(jnp.bfloat16)

    picked = lax.map(one_block, flat_ids.reshape(total // span, span))
    return picked.reshape(total, table.shape[1])


def aggregate(edge_out, targets, segments):
    onehot = (targets[:, None] == jnp.arange(segments, dtype=jnp.int32)[None, :]).astype(
        jnp.bfloat16
    )
    return lax.dot_general(
        onehot, edge_out, (((0,), (0,)), ((), ())), preferred_element_type=jnp.float32
    )


def on_device(
    grid_latent,
    mesh_latent,
    block_owner,
    block_sender,
    block_receiver,
    block_feature,
    mesh_sender,
    mesh_receiver,
    mesh_feature,
    encoder_edge_input,
    encoder_edge_feature,
    encoder_edge_bias,
    encoder_edge_output,
    encoder_edge_gain,
    encoder_node_input,
    encoder_node_bias,
    encoder_node_output,
    encoder_node_gain,
    processor_edge_input,
    processor_edge_feature,
    processor_edge_bias,
    processor_edge_output,
    processor_edge_gain,
    processor_node_input,
    processor_node_bias,
    processor_node_output,
    processor_node_gain,
):
    lon_count = lax.axis_size("lon")
    sub_count = lax.axis_size("sub")
    peer_count = lon_count * sub_count
    rows_lat, rows_lon, channels = mesh_latent.shape
    node_count = rows_lat * rows_lon
    blocks, block_rows = block_sender.shape
    feat_count = block_feature.shape[1]
    mesh_flat = mesh_latent.reshape(node_count, channels)
    mesh_bf = mesh_flat.astype(jnp.bfloat16)
    owner_ids = block_owner[:, 0]
    same_owner = owner_ids[:, None] == owner_ids[None, :]
    earlier = jnp.arange(blocks)[:, None] > jnp.arange(blocks)[None, :]
    order_rank = jnp.sum((same_owner & earlier).astype(jnp.int32), axis=1)
    target_slot = owner_ids * CAP + order_rank
    slot_ids = jnp.arange(peer_count * CAP, dtype=jnp.int32)
    placed = (slot_ids[:, None] == target_slot[None, :]).astype(jnp.int32)
    filled = jnp.sum(placed, axis=1) > 0
    source_block = jnp.sum(placed * jnp.arange(blocks, dtype=jnp.int32)[None, :], axis=1)
    send_index = block_sender[source_block]
    sent_latent = pick_rows(grid_latent, send_index).reshape(peer_count * CAP, block_rows, channels)
    outgoing = jnp.where(filled[:, None, None], sent_latent, jnp.zeros((), jnp.bfloat16))
    targets = jnp.where(filled[:, None], block_receiver[source_block], node_count)
    features = jnp.where(
        filled[:, None, None], block_feature[source_block], jnp.zeros((), jnp.bfloat16)
    )
    sent_rows = lax.all_to_all(
        outgoing.reshape(peer_count, CAP, block_rows, channels),
        ("lon", "sub"),
        split_axis=0,
        concat_axis=0,
        tiled=True,
    )
    node_ids = lax.all_to_all(
        targets.reshape(peer_count, CAP, block_rows),
        ("lon", "sub"),
        split_axis=0,
        concat_axis=0,
        tiled=True,
    )
    edge_feats = lax.all_to_all(
        features.reshape(peer_count, CAP, feat_count, block_rows),
        ("lon", "sub"),
        split_axis=0,
        concat_axis=0,
        tiled=True,
    )
    flat_ids = node_ids.reshape(-1)
    local_rows = pick_rows(mesh_bf, jnp.minimum(flat_ids, node_count - 1))
    feat_rows = jnp.swapaxes(edge_feats, 2, 3).reshape(-1, feat_count)
    edge_out = edge_update(
        sent_rows.reshape(-1, channels),
        local_rows,
        feat_rows,
        encoder_edge_input,
        encoder_edge_feature,
        encoder_edge_bias,
        encoder_edge_output,
        encoder_edge_gain,
    )
    edge_out, node_ids = (edge_out.reshape(sent_rows.shape), node_ids)
    enc_sum = aggregate(edge_out.reshape(-1, channels), node_ids.reshape(-1), node_count)
    mesh_enc = node_update(
        mesh_flat,
        mesh_bf,
        enc_sum,
        encoder_node_input,
        encoder_node_bias,
        encoder_node_output,
        encoder_node_gain,
    )
    enc_bf = mesh_enc.astype(jnp.bfloat16)
    widened = with_halo(
        enc_bf.reshape(rows_lat, rows_lon, channels), ((("lon", "sub"), 1),), W, True
    )
    extended = with_halo(widened, (("lat", 0),), W, False)
    lookup = extended.reshape(-1, channels)
    proc_receivers = mesh_receiver.reshape(-1)
    send_rows = lookup[mesh_sender.reshape(-1)]
    recv_rows = enc_bf[proc_receivers]
    feat_rows = jnp.swapaxes(mesh_feature, 1, 2).reshape(-1, feat_count)
    proc_edges = edge_update(
        send_rows,
        recv_rows,
        feat_rows,
        processor_edge_input,
        processor_edge_feature,
        processor_edge_bias,
        processor_edge_output,
        processor_edge_gain,
    )
    proc_sum = aggregate(proc_edges, proc_receivers, node_count)
    mesh_out = node_update(
        mesh_enc,
        enc_bf,
        proc_sum,
        processor_node_input,
        processor_node_bias,
        processor_node_output,
        processor_node_gain,
    )
    return mesh_out.reshape(rows_lat, rows_lon, channels)


def solution(mesh):
    in_specs = (
        P(("groups", "lon", "lat", "sub"), None),
        P(("groups", "lat"), ("lon", "sub"), None),
        P(("lon", "lat", "sub"), None),
        P(("lon", "lat", "sub"), None),
        P(("lon", "lat", "sub"), None),
        P(("lon", "lat", "sub"), None, None),
        P(("lon", "lat", "sub"), None),
        P(("lon", "lat", "sub"), None),
        P(("lon", "lat", "sub"), None, None),
        P(),
        P(),
        P(),
        P(),
        P(),
        P(),
        P(),
        P(),
        P(),
        P(),
        P(),
        P(),
        P(),
        P(),
        P(),
        P(),
        P(),
        P(),
    )
    out_specs = P(("groups", "lat"), ("lon", "sub"), None)
    return jax.shard_map(
        on_device, mesh=mesh, in_specs=in_specs, out_specs=out_specs, check_vma=False
    )
```

profile of v0, /device:TPU:0, one launch (start us, length us, event | category | flops | bytes accessed | tf_op | source)
XLA Modules:
  0.0 115.6 jit_solution(5895843225290236836)
XLA Ops:
  0.0 0.9 convert_reduce_fusion.1
  0.9 0.7 multiply_add_fusion.1
  1.8 1.3 %gather_fusion = s32[16,128]{1,0:T(8,128)S(1)} fusion(s32[8,128]{1,0:T(8,128)} %param.35, s32[1024]{0:T(1024)S(1)} %pad_clamp_fusion), kind=kCustom, calls=%fused_computation | custom fusion | bytes 16448 | tf_op jit(solution)/shard_map/gather | solution.py:137
  3.0 0.7 broadcast_select_fusion.2
  3.7 6.3 %all-to-all-start = ((s32[8,2,128]{2,1,0:T(2,128)}), s32[8,2,128]{2,1,0:T(2,128)S(1)}, u32[]{:S(2)}, u32[]{:S(2)}) async-start(s32[8,2,128]{2,1,0:T(2,128)} %broadcast_select_fusion.2), calls=%async_computation | async-start | bytes 16384 | tf_op jit(solution)/shard_map/all_to_all | solution.py:148
  10.0 1.2 %gather_fusion.1 = s32[16,128]{1,0:T(8,128)S(1)} fusion(s32[8,128]{1,0:T(8,128)} %param.34, s32[1024]{0:T(1024)S(1)} %pad_clamp_fusion), kind=kCustom, calls=%fused_computation.1 | custom fusion | bytes 16448 | tf_op jit(solution)/shard_map/gather | solution.py:134
  11.4 3.8 %while.22 = (s32[]{:T(128)}, bf16[2,1024,256]{2,1,0:T(8,128)(2,1)S(1)}, s32[2,1024]{1,0:T(2,128)S(1)}, bf16[1024,256]{1,0:T(8,128)(2,1)}, s32[]{:T(128)}) while((s32[]{:T(128)}, bf16[2,1024,256]{2,1,0:T(8,128)(2,1)S(1)}, s32[2,1024]{1,0:T(2,128)S(1)}, bf16[1024,256]{1,0:T(8,128)(2,1)}, s32[]{:T(128)}) %tuple.44), condition=%wide.region_4.5_spmd.clone, body=%wide.region_3.4_spmd.clone.sunk | while | flops 538181632 | bytes 1060933 | solution.py:74
  11.4 1.9 %fusion.97 = bf16[2,1024,256]{2,1,0:T(8,128)(2,1)S(1)} fusion(bf16[2,1024,256]{2,1,0:T(8,128)(2,1)S(1)} %get-tuple-element.167, s32[]{:T(128)} %get-tuple-element.166, bf16[1024,256]{1,0:T(8,128)(2,1)} %get-tuple-element.174, s32[1024]{0:T(1024)S(1)} %bitcast.81), kind=kOutput, calls=%fused_computation.12.clone.1 | convolution fusion | flops 538181632 | bytes 1052676 | tf_op jit(solution)/shard_map/while/body/eval_jaxpr/dot_general | solution.py:72
  13.4 1.9 %fusion.97 = bf16[2,1024,256]{2,1,0:T(8,128)(2,1)S(1)} fusion(bf16[2,1024,256]{2,1,0:T(8,128)(2,1)S(1)} %get-tuple-element.167, s32[]{:T(128)} %get-tuple-element.166, bf16[1024,256]{1,0:T(8,128)(2,1)} %get-tuple-element.174, s32[1024]{0:T(1024)S(1)} %bitcast.81), kind=kOutput, calls=%fused_computation.12.clone.1 | convolution fusion | flops 538181632 | bytes 1052676 | tf_op jit(solution)/shard_map/while/body/eval_jaxpr/dot_general | solution.py:72
  15.3 0.6 gather_fusion.2
  16.0 0.6 copy.36
  16.6 5.1 %all-to-all-start.2 = ((bf16[8,2,4,128]{3,1,2,0:T(2,128)(2,1)}), bf16[8,2,4,128]{3,1,2,0:T(2,128)(2,1)S(1)}, u32[]{:S(2)}, u32[]{:S(2)}) async-start(bf16[8,2,4,128]{3,1,2,0:T(2,128)(2,1)} %copy.36), calls=%async_computation.2 | async-start | bytes 32768 | tf_op jit(solution)/shard_map/all_to_all | solution.py:155
  21.7 1.1 broadcast_select_fusion
  22.9 4.5 %all-to-all-done.2 = bf16[8,2,4,128]{3,1,2,0:T(2,128)(2,1)S(1)} async-done(((bf16[8,2,4,128]{3,1,2,0:T(2,128)(2,1)}), bf16[8,2,4,128]{3,1,2,0:T(2,128)(2,1)S(1)}, u32[]{:S(2)}, u32[]{:S(2)}) %all-to-all-start.2) | async-done | bytes 16416 | tf_op jit(solution)/shard_map/all_to_all | solution.py:155
  27.4 3.6 %all-to-all-start.1 = ((bf16[8,2,128,256]{3,2,1,0:T(8,128)(2,1)}), bf16[8,2,128,256]{3,2,1,0:T(8,128)(2,1)S(1)}, u32[]{:S(2)}, u32[]{:S(2)}) async-start(bf16[8,2,128,256]{3,2,1,0:T(8,128)(2,1)} %broadcast_select_fusion), calls=%async_computation.1 | async-start | bytes 2097152 | tf_op jit(solution)/shard_map/all_to_all | solution.py:141
  31.0 0.6 broadcast_clamp_fusion.1
  31.5 0.6 broadcast_clamp_fusion
  32.5 1.1 while.23
  32.6 0.5 fusion.99
  33.1 0.5 fusion.99
  33.7 0.8 copy.37
  34.5 0.6 reshape.205
  35.1 22.4 %all-to-all-done.1 = bf16[8,2,128,256]{3,2,1,0:T(8,128)(2,1)S(1)} async-done(((bf16[8,2,128,256]{3,2,1,0:T(8,128)(2,1)}), bf16[8,2,128,256]{3,2,1,0:T(8,128)(2,1)S(1)}, u32[]{:S(2)}, u32[]{:S(2)}) %all-to-all-start.1) | async-done | bytes 1048608 | tf_op jit(solution)/shard_map/all_to_all | solution.py:141
  57.5 1.3 %fusion.60 = f32[2048,256]{1,0:T(8,128)S(1)} fusion(bf16[2048,256]{1,0:T(8,128)(2,1)S(1)} %bitcast.78, bf16[512,256]{1,0:T(8,128)(2,1)} %param.40), kind=kOutput, calls=%fused_computation.70 | convolution fusion | flops 268435456 | bytes 3276800 | tf_op jit(solution)/shard_map/dot_general | solution.py:35
  59.5 1.3 %multiply_convert_fusion.3 = bf16[2048,256]{1,0:T(8,128)(2,1)S(1)} fusion(f32[2048,256]{1,0:T(8,128)S(1)} %convolution_add_fusion.3, bf16[2048,4]{0,1:T(4,128)(2,1)S(1)} %copy-done.14, f32[4,256]{1,0:T(4,128)S(1)} %copy-done.18, f32[256]{0:T(256)S(1)} %copy-done.20), kind=kOutput, calls=%fused_computation.39 | convolution fusion | flops 28835840 | bytes 3167232 | tf_op jit(solution)/shard_map/dot_general | solution.py:41
  61.7 0.6 add_rsqrt_fusion.1
  62.3 2.5 %multiply_convert_fusion.11 = bf16[512,256]{1,0:T(8,128)(2,1)S(1)} fusion(f32[512,256]{1,0:T(8,128)S(1)} %fusion.62, s32[2048]{0:T(1024)S(1)} %bitcast.86, f32[2048,256]{0,1:T(8,128)S(1)} %get-tuple-element.104, f32[256]{0:T(256)} %param.44, f32[2048]{0:T(1024)} %add_rsqrt_fusion.1, f32[2048]{0:T(1024)S(1)} %broadcast_multiply_fusion.1, f32[256]{0:T(256)} %param.46, ...), kind=kOutput, calls=%fused_computation.60 | convolution fusion | flops 609222656 | bytes 3041280 | tf_op jit(solution)/shard_map/dot_general | solution.py:54
  64.8 1.2 %fusion.70 = (f32[512]{0:T(512)S(1)}, f32[512,256]{1,0:T(8,128)S(1)}) fusion(bf16[512,256]{1,0:T(8,128)(2,1)S(1)} %multiply_convert_fusion.11, bf16[256,256]{1,0:T(8,128)(2,1)} %param.47), kind=kOutput, calls=%fused_computation.107 | convolution fusion | flops 67239424 | bytes 919552 | tf_op jit(solution)/shard_map/dot_general | solution.py:60
  66.3 0.9 fusion.67
  67.2 0.6 fusion.68
  67.8 3.5 %collective-permute-start.1 = (bf16[8,2,256]{2,1,0:T(2,128)(2,1)}, bf16[8,2,256]{2,1,0:T(2,128)(2,1)}, u32[]{:S(2)}, u32[]{:S(2)}) collective-permute-start(bf16[8,2,256]{2,1,0:T(2,128)(2,1)} %get-tuple-element.102), channel_id=1, source_target_pairs={{1,0},{4,1},{5,4},{8,5},{9,8},{12,9},{13,12},{0,13},{3,2},{6,3},{7... | collective-permute-start | bytes 24584 | tf_op jit(solution)/shard_map/ppermute | solution.py:20
  71.3 9.0 %gather_fusion.4 = bf16[2048,256]{1,0:T(8,128)(2,1)} fusion(bf16[512,256]{1,0:T(8,128)(2,1)S(1)} %fusion.67, s32[2048]{0:T(1024)S(1)} %copy-done.13), kind=kCustom, calls=%fused_computation.4 | custom fusion | bytes 2105344 | tf_op jit(solution)/shard_map/gather | solution.py:194
  80.4 1.7 %fusion.53 = f32[2048,256]{1,0:T(8,128)S(1)} fusion(bf16[2048,256]{1,0:T(8,128)(2,1)} %gather_fusion.4, bf16[512,256]{1,0:T(8,128)(2,1)S(1)} %copy-done.4), kind=kOutput, calls=%fused_computation.63 | convolution fusion | flops 268435456 | bytes 3276800 | tf_op jit(solution)/shard_map/dot_general | solution.py:36
  82.1 0.7 pad_maximum_fusion.3
  82.8 3.4 %collective-permute-start.2 = (bf16[2,68,256]{2,1,0:T(8,128)(2,1)S(1)}, bf16[2,68,256]{2,1,0:T(8,128)(2,1)S(1)}, u32[]{:S(2)}, u32[]{:S(2)}) collective-permute-start(bf16[2,68,256]{2,1,0:T(8,128)(2,1)S(1)} %get-tuple-element.99), channel_id=1, source_target_pairs={{0,2},{1,3},{4,6},{5,7},{8,10},{9,11},{12,14},{13,15},{16,18},{17,... | collective-permute-start | bytes 208904 | tf_op jit(solution)/shard_map/ppermute | solution.py:19
  86.2 1.5 %collective-permute-start.3 = (bf16[2,68,256]{2,1,0:T(8,128)(2,1)S(1)}, bf16[2,68,256]{2,1,0:T(8,128)(2,1)S(1)}, u32[]{:S(2)}, u32[]{:S(2)}) collective-permute-start(bf16[2,68,256]{2,1,0:T(8,128)(2,1)S(1)} %get-tuple-element.100), channel_id=1, source_target_pairs={{2,0},{3,1},{6,4},{7,5},{10,8},{11,9},{14,12},{15,13},{18,16},{19,... | collective-permute-start | bytes 208904 | tf_op jit(solution)/shard_map/ppermute | solution.py:20
  87.7 1.0 fusion.56
  88.8 3.7 %collective-permute-done.3 = bf16[2,68,256]{2,1,0:T(8,128)(2,1)S(1)} collective-permute-done((bf16[2,68,256]{2,1,0:T(8,128)(2,1)S(1)}, bf16[2,68,256]{2,1,0:T(8,128)(2,1)S(1)}, u32[]{:S(2)}, u32[]{:S(2)}) %collective-permute-start.3) | collective-permute-done | bytes 69664 | tf_op jit(solution)/shard_map/ppermute | solution.py:20
  92.5 1.5 %pad_maximum_fusion = bf16[12,68,256]{2,1,0:T(8,128)(2,1)} fusion(bf16[2,68,256]{2,1,0:T(8,128)(2,1)S(1)} %collective-permute-done.3, bf16[8,2,256]{2,1,0:T(2,128)(2,1)} %collective-permute-done.1, bf16[8,64,256]{2,1,0:T(8,128)(2,1)S(1)} %bitcast.77, bf16[8,2,256]{2,1,0:T(2,128)(2,1)S(1)} %collective-permute-done, ...), kind=kLoop, calls=%fused_computation.61 | loop fusion | flops 2088960 | bytes 835584 | tf_op jit(solution)/shard_map/concatenate | solution.py:21
  94.0 1.1 reshape.207
  95.1 9.9 %gather_fusion.3 = bf16[2048,256]{1,0:T(8,128)(2,1)} fusion(bf16[816,256]{1,0:T(8,128)(2,1)S(1)} %reshape.207, s32[2048]{0:T(1024)} %broadcast_clamp_fusion.1), kind=kCustom, calls=%fused_computation.3 | custom fusion | bytes 2105344 | tf_op jit(solution)/shard_map/gather | solution.py:193
  105.1 1.7 %convolution_add_fusion.2 = f32[2048,256]{1,0:T(8,128)S(1)} fusion(f32[2048,256]{1,0:T(8,128)S(1)} %fusion.53, bf16[2048,256]{1,0:T(8,128)(2,1)} %gather_fusion.3, bf16[512,256]{1,0:T(8,128)(2,1)S(1)} %copy-done.5), kind=kOutput, calls=%fused_computation.29 | convolution fusion | flops 268959744 | bytes 5373952 | tf_op jit(solution)/shard_map/dot_general | solution.py:35
  106.8 1.4 %multiply_convert_fusion.1 = bf16[2048,256]{1,0:T(8,128)(2,1)S(1)} fusion(f32[2048,256]{1,0:T(8,128)S(1)} %convolution_add_fusion.2, f32[4,256]{1,0:T(4,128)S(1)} %copy-done.19, f32[256]{0:T(256)S(1)} %copy-done.21, bf16[16,4,128]{2,1,0:T(4,128)(2,1)S(1)} %copy-done.17), kind=kOutput, calls=%fused_computation.35 | convolution fusion | flops 28835840 | bytes 3167232 | tf_op jit(solution)/shard_map/dot_general | solution.py:41
  108.2 0.5 fusion.71
  108.9 0.6 add_rsqrt_fusion
  109.5 2.7 %multiply_convert_fusion.8 = bf16[512,256]{1,0:T(8,128)(2,1)S(1)} fusion(f32[512,256]{1,0:T(8,128)} %fusion.56, s32[2048]{0:T(1024)} %bitcast.90, f32[2048,256]{0,1:T(8,128)S(1)} %get-tuple-element.108, f32[256]{0:T(256)} %param.53, f32[2048]{0:T(1024)} %add_rsqrt_fusion, f32[2048]{0:T(1024)S(1)} %broadcast_multiply_fusion, f32[256]{0:T(256)} %param.55, ...), kind=kOutput, calls=%fused_computation.58 | convolution fusion | flops 609222656 | bytes 3041280 | tf_op jit(solution)/shard_map/dot_general | solution.py:54
  112.3 1.2 %fusion.72 = (f32[512]{0:T(512)S(1)}, f32[512,256]{1,0:T(8,128)S(1)}) fusion(bf16[512,256]{1,0:T(8,128)(2,1)S(1)} %multiply_convert_fusion.8, bf16[256,256]{1,0:T(8,128)(2,1)} %param.56), kind=kOutput, calls=%fused_computation.109 | convolution fusion | flops 67239424 | bytes 919552 | tf_op jit(solution)/shard_map/dot_general | solution.py:60
  113.8 1.8 %multiply_add_fusion = f32[512,256]{1,0:T(8,128)} fusion(f32[512,256]{1,0:T(8,128)S(1)} %get-tuple-element.110, f32[256]{0:T(256)} %param.57, f32[512]{0:T(512)S(1)} %add_rsqrt_fusion.2, f32[512]{0:T(512)S(1)} %broadcast_multiply_fusion.2, f32[256]{0:T(256)} %param.48, f32[512]{0:T(512)S(1)} %add_rsqrt_fusion.3, f32[512,256]{1,0:T(8,128)S(1)} %get-tuple-element.106, ...), kind=kLoop, calls=%fused_computation.56 | loop fusion | flops 1048576 | bytes 2107392 | tf_op jit(solution)/shard_map/add | solution.py:61
  (81 shorter events, 3.1 us)
Async XLA Ops:
  0.0 60.9 %copy-start = (bf16[256,256]{1,0:T(8,128)(2,1)S(1)}, bf16[256,256]{1,0:T(8,128)(2,1)}, u32[]{:S(2)}) copy-start(bf16[256,256]{1,0:T(8,128)(2,1)} %param.43) | copy-start | bytes 393220
  3.7 12.9 %all-to-all-start = ((s32[8,2,128]{2,1,0:T(2,128)}), s32[8,2,128]{2,1,0:T(2,128)S(1)}, u32[]{:S(2)}, u32[]{:S(2)}) async-start(s32[8,2,128]{2,1,0:T(2,128)} %broadcast_select_fusion.2), calls=%async_computation | async-start | bytes 16384 | tf_op jit(solution)/shard_map/all_to_all | solution.py:148
  11.4 3.9 %copy-start.10 = (bf16[8,4,128]{2,1,0:T(4,128)(2,1)S(1)}, bf16[8,4,128]{2,1,0:T(4,128)(2,1)}, u32[]{:S(2)}) copy-start(bf16[8,4,128]{2,1,0:T(4,128)(2,1)} %param.36) | copy-start | bytes 24580
  11.4 4.5 %copy-start.15 = (s32[16,128]{1,0:T(8,128)S(1)}, s32[16,128]{1,0:T(8,128)}, u32[]{:S(2)}) copy-start(s32[16,128]{1,0:T(8,128)} %param.37) | copy-start | bytes 24580
  11.4 4.5 %copy-start.16 = (s32[16,128]{1,0:T(8,128)S(1)}, s32[16,128]{1,0:T(8,128)}, u32[]{:S(2)}) copy-start(s32[16,128]{1,0:T(8,128)} %param.38) | copy-start | bytes 24580
  16.6 15.8 %copy-start.11 = (s32[8,2,128]{2,1,0:T(2,128)}, s32[8,2,128]{2,1,0:T(2,128)S(1)}, u32[]{:S(2)}) copy-start(s32[8,2,128]{2,1,0:T(2,128)S(1)} %all-to-all-done) | copy-start | bytes 24580
  16.6 10.8 %all-to-all-start.2 = ((bf16[8,2,4,128]{3,1,2,0:T(2,128)(2,1)}), bf16[8,2,4,128]{3,1,2,0:T(2,128)(2,1)S(1)}, u32[]{:S(2)}, u32[]{:S(2)}) async-start(bf16[8,2,4,128]{3,1,2,0:T(2,128)(2,1)} %copy.36), calls=%async_computation.2 | async-start | bytes 32768 | tf_op jit(solution)/shard_map/all_to_all | solution.py:155
  21.7 10.4 %copy-start.1 = (f32[8,64,256]{2,1,0:T(8,128)S(1)}, f32[8,64,256]{2,1,0:T(8,128)}, u32[]{:S(2)}) copy-start(f32[8,64,256]{2,1,0:T(8,128)} %param.32) | copy-start | bytes 1572868
  21.7 10.4 %copy-start.7 = (bf16[512,256]{1,0:T(8,128)(2,1)S(1)}, bf16[512,256]{1,0:T(8,128)(2,1)}, u32[]{:S(2)}) copy-start(bf16[512,256]{1,0:T(8,128)(2,1)} %param.45) | copy-start | bytes 786436
  27.4 5.1 %copy-start.9 = (bf16[8,2,4,128]{3,1,2,0:T(2,128)(2,1)}, bf16[8,2,4,128]{3,1,2,0:T(2,128)(2,1)S(1)}, u32[]{:S(2)}) copy-start(bf16[8,2,4,128]{3,1,2,0:T(2,128)(2,1)S(1)} %all-to-all-done.2) | copy-start | bytes 49156
  27.4 30.1 %all-to-all-start.1 = ((bf16[8,2,128,256]{3,2,1,0:T(8,128)(2,1)}), bf16[8,2,128,256]{3,2,1,0:T(8,128)(2,1)S(1)}, u32[]{:S(2)}, u32[]{:S(2)}) async-start(bf16[8,2,128,256]{3,2,1,0:T(8,128)(2,1)} %broadcast_select_fusion), calls=%async_computation.1 | async-start | bytes 2097152 | tf_op jit(solution)/shard_map/all_to_all | solution.py:141
  33.7 25.1 %copy-start.3 = (bf16[512,256]{1,0:T(8,128)(2,1)S(1)}, bf16[512,256]{1,0:T(8,128)(2,1)}, u32[]{:S(2)}) copy-start(bf16[512,256]{1,0:T(8,128)(2,1)} %param.40) | copy-start | bytes 786436
  58.8 0.7 copy-start.14
  58.8 0.7 copy-start.18
  58.8 0.7 copy-start.20
  60.9 1.4 %copy-start.12 = (s32[8,2,128]{2,1,0:T(2,128)S(1)}, s32[8,2,128]{2,1,0:T(2,128)}, u32[]{:S(2)}) copy-start(s32[8,2,128]{2,1,0:T(2,128)} %copy-done.11) | copy-start | bytes 24580
  64.7 6.6 %copy-start.13 = (s32[2048]{0:T(1024)S(1)}, s32[2048]{0:T(1024)}, u32[]{:S(2)}) copy-start(s32[2048]{0:T(1024)} %broadcast_clamp_fusion) | copy-start | bytes 24580
  67.8 14.3 %collective-permute-start = (bf16[8,2,256]{2,1,0:T(2,128)(2,1)}, bf16[8,2,256]{2,1,0:T(2,128)(2,1)S(1)}, u32[]{:S(2)}, u32[]{:S(2)}) collective-permute-start(bf16[8,2,256]{2,1,0:T(2,128)(2,1)} %get-tuple-element.101), channel_id=1, source_target_pairs={{0,1},{1,4},{4,5},{5,8},{8,9},{9,12},{12,13},{13,0},{2,3},{3,6},{6... | collective-permute-start | bytes 24584 | tf_op jit(solution)/shard_map/ppermute | solution.py:19
  67.8 12.6 %copy-start.4 = (bf16[512,256]{1,0:T(8,128)(2,1)S(1)}, bf16[512,256]{1,0:T(8,128)(2,1)}, u32[]{:S(2)}) copy-start(bf16[512,256]{1,0:T(8,128)(2,1)} %param.49) | copy-start | bytes 786436
  67.8 14.3 %collective-permute-start.1 = (bf16[8,2,256]{2,1,0:T(2,128)(2,1)}, bf16[8,2,256]{2,1,0:T(2,128)(2,1)}, u32[]{:S(2)}, u32[]{:S(2)}) collective-permute-start(bf16[8,2,256]{2,1,0:T(2,128)(2,1)} %get-tuple-element.102), channel_id=1, source_target_pairs={{1,0},{4,1},{5,4},{8,5},{9,8},{12,9},{13,12},{0,13},{3,2},{6,3},{7... | collective-permute-start | bytes 24584 | tf_op jit(solution)/shard_map/ppermute | solution.py:20
  80.4 7.3 %copy-start.8 = (bf16[512,256]{1,0:T(8,128)(2,1)S(1)}, bf16[512,256]{1,0:T(8,128)(2,1)}, u32[]{:S(2)}) copy-start(bf16[512,256]{1,0:T(8,128)(2,1)} %param.54) | copy-start | bytes 786436
  82.8 5.9 %collective-permute-start.2 = (bf16[2,68,256]{2,1,0:T(8,128)(2,1)S(1)}, bf16[2,68,256]{2,1,0:T(8,128)(2,1)S(1)}, u32[]{:S(2)}, u32[]{:S(2)}) collective-permute-start(bf16[2,68,256]{2,1,0:T(8,128)(2,1)S(1)} %get-tuple-element.99), channel_id=1, source_target_pairs={{0,2},{1,3},{4,6},{5,7},{8,10},{9,11},{12,14},{13,15},{16,18},{17,... | collective-permute-start | bytes 208904 | tf_op jit(solution)/shard_map/ppermute | solution.py:19
  86.2 6.2 %collective-permute-start.3 = (bf16[2,68,256]{2,1,0:T(8,128)(2,1)S(1)}, bf16[2,68,256]{2,1,0:T(8,128)(2,1)S(1)}, u32[]{:S(2)}, u32[]{:S(2)}) collective-permute-start(bf16[2,68,256]{2,1,0:T(8,128)(2,1)S(1)} %get-tuple-element.100), channel_id=1, source_target_pairs={{2,0},{3,1},{6,4},{7,5},{10,8},{11,9},{14,12},{15,13},{18,16},{19,... | collective-permute-start | bytes 208904 | tf_op jit(solution)/shard_map/ppermute | solution.py:20
  95.1 9.9 %copy-start.5 = (bf16[512,256]{1,0:T(8,128)(2,1)S(1)}, bf16[512,256]{1,0:T(8,128)(2,1)}, u32[]{:S(2)}) copy-start(bf16[512,256]{1,0:T(8,128)(2,1)} %param.49) | copy-start | bytes 786436
  105.0 1.7 %copy-start.17 = (bf16[16,4,128]{2,1,0:T(4,128)(2,1)S(1)}, bf16[16,4,128]{2,1,0:T(4,128)(2,1)}, u32[]{:S(2)}) copy-start(bf16[16,4,128]{2,1,0:T(4,128)(2,1)} %param.39) | copy-start | bytes 49156
  105.0 1.7 %copy-start.19 = (f32[4,256]{1,0:T(4,128)S(1)}, f32[4,256]{1,0:T(4,128)}, u32[]{:S(2)}) copy-start(f32[4,256]{1,0:T(4,128)} %param.50) | copy-start | bytes 12292
  105.0 1.7 %copy-start.21 = (f32[256]{0:T(256)S(1)}, f32[256]{0:T(256)}, u32[]{:S(2)}) copy-start(f32[256]{0:T(256)} %param.51) | copy-start | bytes 3076
  106.8 1.4 %copy-start.6 = (bf16[256,256]{1,0:T(8,128)(2,1)S(1)}, bf16[256,256]{1,0:T(8,128)(2,1)}, u32[]{:S(2)}) copy-start(bf16[256,256]{1,0:T(8,128)(2,1)} %param.52) | copy-start | bytes 393220
  109.5 4.3 %copy-start.2 = (f32[8,64,256]{2,1,0:T(8,128)S(1)}, f32[8,64,256]{2,1,0:T(8,128)}, u32[]{:S(2)}) copy-start(f32[8,64,256]{2,1,0:T(8,128)} %param.32) | copy-start | bytes 1572868
where the time goes:
time: 117 us; the launch traced here: 116 us
  waiting for transfers between devices  30.7 us (26%)
  local copies, waits for them, and re-layouts  26.4 us (23%)
  starting transfers between devices  23.4 us (20%)
  matrix products  22.6 us (19%)
  other arithmetic  12 us (10%)
    all_to_all x1, waiting for transfers between devices, on_device(): lax.all_to_all(outgoing.reshape(peer_count, CAP, block_rows, channels), (...  22.4 us
    gather x1, local copies, waits for them, and re-layouts, on_device(): send_rows = lookup[mesh_sender.reshape(-1)]  9.91 us
    gather x1, local copies, waits for them, and re-layouts, on_device(): recv_rows = enc_bf[proc_receivers]  9.03 us
    all_to_all x1, starting transfers between devices, on_device(): lax.all_to_all(targets.reshape(peer_count, CAP, block_rows), ('lon', 'sub...  6.33 us
    dot_general x2, matrix products, node_update(): jnp.dot(summed.astype(jnp.bfloat16), input_weight[channels:], preferred_e...  5.2 us
    all_to_all x1, starting transfers between devices, on_device(): lax.all_to_all(features.reshape(peer_count, CAP, feat_count, block_rows),...  5.1 us
    ppermute x2, starting transfers between devices, with_halo(): after = lax.ppermute(first, axis, down)  5.01 us
    dot_general x4, matrix products, one_block(): jnp.dot(selector, table, preferred_element_type=jnp.float32)  4.81 us
  transfers between devices with their start and end apart: 7, of which 3 were waited for; matrix products, arithmetic and copies ran while one was open for 20% of the time, Pallas kernels for 0%

commit v1 on v0

v1 whole, which is shorter than its diff:
```python
import functools

import jax
import jax.numpy as jnp
from jax import lax
from jax.experimental import pallas as pl
from jax.experimental.pallas import tpu as pltpu
from jax.sharding import PartitionSpec as P

CAP = 2
W = 2
MESH = pl.DeviceIdType.MESH
BF = jnp.bfloat16
F32 = jnp.float32


def dot(a, b):
    return jnp.dot(a, b, preferred_element_type=F32)


def silu(v):
    half = 0.5 * v
    return half + half * jnp.tanh(half)


def layer_norm(values, gain):
    center = values - jnp.mean(values, axis=-1, keepdims=True)
    spread = jnp.mean(center * center, axis=-1, keepdims=True)
    return center * lax.rsqrt(spread + 1e-05) * gain


def one_hot(match):
    return jnp.where(match, 1.0, 0.0).astype(BF)


def split3(w):
    a = w.astype(BF)
    r = w - a.astype(F32)
    b = r.astype(BF)
    c = (r - b.astype(F32)).astype(BF)
    return a, b, c


def feature_term(feat_t, w_ref):
    total = feat_t[:, 0:1] * w_ref[0:1, :]
    for f in range(1, w_ref.shape[0]):
        total = total + feat_t[:, f : f + 1] * w_ref[f : f + 1, :]
    return total


def kernel(
    peers,
    subs,
    lats,
    grid_ref,
    mesh_ref,
    owner_ref,
    bsend_ref,
    brecv_ref,
    bfeat_ref,
    msend_ref,
    mrecv_ref,
    mfeat_ref,
    eei,
    eef,
    eeb,
    eeo,
    eeg,
    eni,
    enb,
    eno,
    eng,
    pei,
    pef,
    peb,
    peo,
    peg,
    pni,
    pnb,
    pno,
    png,
    out_ref,
    gproj,
    blkpre,
    send,
    meta_s,
    recv,
    meta_r,
    acc,
    ptab,
    table,
    packs,
    halo_rows,
    halo_packs,
    menc,
    oh,
    oht,
    fbase,
    send_sem,
    recv_sem,
    msend_sem,
    mrecv_sem,
    hsend_sem,
    hrecv_sem,
):
    grid_rows, ch = grid_ref.shape
    nodes = mesh_ref.shape[0]
    blocks, eb = bsend_ref.shape
    pblocks = msend_ref.shape[0]
    feats = bfeat_ref.shape[1]
    pair = CAP * eb
    lon = lax.axis_index("lon")
    lat = lax.axis_index("lat")
    sub = lax.axis_index("sub")
    me = lon * subs + sub
    half = peers // 2

    def at(p, l=None):
        p = lax.rem(p + 2 * peers, peers)
        place = {"lon": p // subs, "sub": lax.rem(p, subs)}
        if l is not None:
            place["lat"] = l
        return place

    barrier = pltpu.get_barrier_semaphore()

    def greet(k, carry):
        pl.semaphore_signal(barrier, inc=1, device_id=at(me + k), device_id_type=MESH)
        return carry

    lax.fori_loop(1, peers, greet, 0)
    for dl in (-1, 1):

        @pl.when((lat + dl >= 0) & (lat + dl < lats))
        def _():
            for dp in (-1, 0, 1):
                pl.semaphore_signal(
                    barrier, inc=1, device_id=at(me + dp, lat + dl), device_id_type=MESH
                )

    gproj[...] = dot(grid_ref[...], eei[:ch, :]).astype(BF)
    send_t = bsend_ref[...].astype(F32).T.astype(jnp.int32)
    lane_g = lax.broadcasted_iota(jnp.int32, (eb, grid_rows), 1)
    for b in range(blocks):
        picked = dot(one_hot(send_t[:, b : b + 1] == lane_g), gproj[...])
        feat_t = bfeat_ref[b].astype(F32).T
        blkpre[b] = (picked + feature_term(feat_t, eef) + eeb[...]).astype(BF)

    bands = jnp.where(lat > 0, 1, 0) + jnp.where(lat < lats - 1, 1, 0)
    pl.semaphore_wait(barrier, peers - 1 + 3 * bands)

    def offset(i):
        return jnp.where(lax.rem(i, 2) == 0, half + i // 2, half - (i + 1) // 2)

    def fill(k):
        q = lax.rem(me + k, peers)
        n = jnp.int32(0)
        s0 = jnp.int32(0)
        s1 = jnp.int32(0)
        for b in range(blocks):
            m = owner_ref[b, 0] == q
            s0 = jnp.where(m & (n == 0), b, s0)
            s1 = jnp.where(m & (n == 1), b, s1)
            n = n + m.astype(jnp.int32)
        send[k, 0:eb, :] = blkpre[s0]
        send[k, eb:pair, :] = blkpre[s1]
        r0 = brecv_ref[pl.ds(s0, 1), :]
        r1 = brecv_ref[pl.ds(s1, 1), :]
        meta_s[k, 0:1, :] = jnp.where(n > 0, r0, nodes)
        meta_s[k, 1:2, :] = jnp.where(n > 1, r1, nodes)
        meta_s[k, 2:8, :] = jnp.full((6, eb), nodes, jnp.int32)

    def copies(k):
        data = pltpu.make_async_remote_copy(
            src_ref=send.at[k],
            dst_ref=recv.at[k],
            send_sem=send_sem.at[k],
            recv_sem=recv_sem.at[k],
            device_id=at(me + k),
            device_id_type=MESH,
        )
        meta = pltpu.make_async_remote_copy(
            src_ref=meta_s.at[k],
            dst_ref=meta_r.at[k],
            send_sem=msend_sem.at[k],
            recv_sem=mrecv_sem.at[k],
            device_id=at(me + k),
            device_id_type=MESH,
        )
        return data, meta

    def send_step(i, carry):
        k = offset(i)
        fill(k)
        data, meta = copies(k)
        meta.start()
        data.start()
        return carry

    lax.fori_loop(0, peers - 1, send_step, 0)
    fill(0)

    mesh_bf = mesh_ref[...].astype(BF)
    ptab[...] = dot(mesh_bf, eei[ch:, :]).astype(BF)
    acc[...] = jnp.zeros_like(acc)
    cells = 68
    rows = nodes // 64
    s = msend_ref[...]
    a = lax.shift_right_logical(s * 241, 14)
    b_ = s - a * cells - W
    a = a - W
    above = a < 0
    below = a >= rows
    row_id = jnp.where(above, a + rows + W, jnp.where(below, a + W, a))
    local = jnp.where(above, a + rows, jnp.where(below, a - rows, a))
    which = jnp.where(above, 0, jnp.where(below, 2, 1))
    base = nodes + 2 * W * 64
    left = b_ < 0
    inner = (~left) & (b_ < 64)
    side = jnp.where(left, 0, 3)
    bb = jnp.where(left, b_ + W, b_ - 64)
    cell = jnp.where(inner, row_id * 64 + b_, base + (side + which) * 16 + local * W + bb)
    cell_t = cell.astype(F32).T.astype(jnp.int32)
    mrecv = mrecv_ref[...]
    recv_base = base + 96
    mrecv_t = (mrecv + recv_base).astype(F32).T.astype(jnp.int32)
    width = table.shape[0]
    lane_t = lax.broadcasted_iota(jnp.int32, (eb, width), 1)
    sub_n = lax.broadcasted_iota(jnp.int32, (nodes, eb), 0)
    for b in range(pblocks):
        hit = (cell_t[:, b : b + 1] == lane_t) | (mrecv_t[:, b : b + 1] == lane_t)
        oh[pl.ds(b * eb, eb), :] = one_hot(hit)
        oht[:, pl.ds(b * eb, eb)] = one_hot(sub_n == mrecv[b : b + 1, :])
        feat_t = mfeat_ref[b].astype(F32).T
        fbase[pl.ds(b * eb, eb), :] = feature_term(feat_t, pef) + peb[...]

    lane_n = lax.broadcasted_iota(jnp.int32, (eb, nodes), 1)

    def encode(data, meta):
        ids = meta[...]
        ids_t = ids.astype(F32).T.astype(jnp.int32)
        parts = []
        for j in range(CAP):
            picked = dot(one_hot(ids_t[:, j : j + 1] == lane_n), ptab[...])
            pre = picked + data[pl.ds(j * eb, eb), :].astype(F32)
            parts.append(silu(pre).astype(BF))
        hidden = jnp.concatenate(parts, axis=0)
        edges = layer_norm(dot(hidden, eeo[...]), eeg[...]).astype(BF)
        spread = jnp.concatenate(
            [one_hot(sub_n == ids[j : j + 1, :]) for j in range(CAP)], axis=1
        )
        acc[...] += dot(spread, edges)

    encode(send.at[0], meta_s.at[0])

    def recv_step(i, carry):
        k = offset(i)
        data, meta = copies(k)
        meta.wait()
        data.wait()
        encode(recv.at[k], meta_r.at[k])
        return carry

    lax.fori_loop(0, peers - 1, recv_step, 0)

    def node(own_bf, summed, w_in, bias, w_out, gain):
        pre = dot(own_bf, w_in[:ch, :]) + dot(summed.astype(BF), w_in[ch:, :]) + bias[...]
        return layer_norm(dot(silu(pre).astype(BF), w_out[...]), gain[...])

    mesh_enc = mesh_ref[...] + node(mesh_bf, acc[...], eni, enb, eno, eng)
    menc[...] = mesh_enc
    enc_bf = mesh_enc.astype(BF)
    own = dot(enc_bf, pei[:ch, :]).astype(BF)
    table[0:nodes, :] = own
    pick_r = lax.broadcasted_iota(jnp.int32, (32, nodes), 0)
    pick_n = lax.broadcasted_iota(jnp.int32, (32, nodes), 1)
    r16 = pick_r & 15
    wanted = (r16 >> 1) * 64 + (r16 & 1) + jnp.where(pick_r < 16, 62, 0)
    packed = dot(one_hot(wanted == pick_n), own).astype(BF)
    packs[0] = packed[0:16]
    packs[1] = packed[16:32]

    edge = W * 64

    def side_copy(dp, dl):
        n = (0 if dp == 1 else 3) + (1 - dl)
        return pltpu.make_async_remote_copy(
            src_ref=packs.at[0 if dp == 1 else 1],
            dst_ref=halo_packs.at[n],
            send_sem=hsend_sem.at[n],
            recv_sem=hrecv_sem.at[n],
            device_id=at(me + dp, lat + dl),
            device_id_type=MESH,
        )

    def band_copy(dl):
        n = 0 if dl == 1 else 1
        first = nodes - edge if dl == 1 else 0
        return pltpu.make_async_remote_copy(
            src_ref=table.at[pl.ds(first, edge), :],
            dst_ref=halo_rows.at[n],
            send_sem=hsend_sem.at[6 + n],
            recv_sem=hrecv_sem.at[6 + n],
            device_id=at(me, lat + dl),
            device_id_type=MESH,
        )

    def inside(dl):
        return (lat + dl >= 0) & (lat + dl < lats)

    for dl in (-1, 1):

        @pl.when(inside(dl))
        def _():
            band_copy(dl).start()
            side_copy(1, dl).start()
            side_copy(-1, dl).start()

    side_copy(1, 0).start()
    side_copy(-1, 0).start()
    table[recv_base : recv_base + nodes, :] = dot(enc_bf, pei[ch:, :]).astype(BF)
    table[recv_base + nodes :, :] = jnp.zeros((width - recv_base - nodes, ch), BF)
    own_in = dot(enc_bf, pni[:ch, :]) + pnb[...]

    for dl in (-1, 1):
        n = 0 if dl == -1 else 1
        slots = (0, 3) if dl == -1 else (2, 5)

        @pl.when(inside(dl))
        def _():
            band_copy(-dl).wait_recv()
            side_copy(1, -dl).wait_recv()
            side_copy(-1, -dl).wait_recv()
            table[pl.ds(nodes + n * edge, edge), :] = halo_rows[n]
            for m in slots:
                table[pl.ds(base + m * 16, 16), :] = halo_packs[m]

        @pl.when(jnp.logical_not(inside(dl)))
        def _():
            table[pl.ds(nodes + n * edge, edge), :] = jnp.zeros((edge, ch), BF)
            for m in slots:
                table[pl.ds(base + m * 16, 16), :] = jnp.zeros((16, ch), BF)

    side_copy(1, 0).wait_recv()
    side_copy(-1, 0).wait_recv()
    table[pl.ds(base + 16, 16), :] = halo_packs[1]
    table[pl.ds(base + 64, 16), :] = halo_packs[4]

    acc[...] = jnp.zeros_like(acc)
    step = 4 * eb

    def process(i, carry):
        first = pl.multiple_of(i * step, step)
        pre = dot(oh[pl.ds(first, step), :], table[...]) + fbase[pl.ds(first, step), :]
        hidden = silu(pre).astype(BF)
        edges = layer_norm(dot(hidden, peo[...]), peg[...]).astype(BF)
        acc[...] += dot(oht[:, pl.ds(first, step)], edges)
        return carry

    lax.fori_loop(0, pblocks * eb // step, process, 0)
    pre = own_in + dot(acc[...].astype(BF), pni[ch:, :])
    out_ref[...] = menc[...] + layer_norm(dot(silu(pre).astype(BF), pno[...]), png[...])

    for dl in (-1, 1):

        @pl.when(inside(dl))
        def _():
            band_copy(dl).wait_send()
            side_copy(1, dl).wait_send()
            side_copy(-1, dl).wait_send()

    side_copy(1, 0).wait_send()
    side_copy(-1, 0).wait_send()


def on_device(
    grid_latent,
    mesh_latent,
    block_owner,
    block_sender,
    block_receiver,
    block_feature,
    mesh_sender,
    mesh_receiver,
    mesh_feature,
    *weights,
):
    subs = lax.axis_size("sub")
    peers = lax.axis_size("lon") * subs
    lats = lax.axis_size("lat")
    rows_lat, rows_lon, ch = mesh_latent.shape
    nodes = rows_lat * rows_lon
    blocks, eb = block_sender.shape
    pblocks = mesh_sender.shape[0]
    weights = [w.reshape(1, -1) if w.ndim == 1 else w for w in weights]
    width = 1408
    vm = pl.BlockSpec(memory_space=pltpu.VMEM)
    sm = pl.BlockSpec(memory_space=pltpu.SMEM)
    dma = pltpu.SemaphoreType.DMA
    out = pl.pallas_call(
        functools.partial(kernel, peers, subs, lats),
        out_shape=jax.ShapeDtypeStruct((nodes, ch), F32),
        in_specs=[vm, vm, sm] + [vm] * (6 + len(weights)),
        out_specs=vm,
        scratch_shapes=[
            pltpu.VMEM(grid_latent.shape, BF),
            pltpu.VMEM((blocks, eb, ch), BF),
            pltpu.VMEM((peers, CAP * eb, ch), BF),
            pltpu.VMEM((peers, 8, eb), jnp.int32),
            pltpu.VMEM((peers, CAP * eb, ch), BF),
            pltpu.VMEM((peers, 8, eb), jnp.int32),
            pltpu.VMEM((nodes, ch), F32),
            pltpu.VMEM((nodes, ch), BF),
            pltpu.VMEM((width, ch), BF),
            pltpu.VMEM((2, 16, ch), BF),
            pltpu.VMEM((2, W * rows_lon, ch), BF),
            pltpu.VMEM((6, 16, ch), BF),
            pltpu.VMEM((nodes, ch), F32),
            pltpu.VMEM((pblocks * eb, width), BF),
            pltpu.VMEM((nodes, pblocks * eb), BF),
            pltpu.VMEM((pblocks * eb, ch), F32),
            dma((peers,)),
            dma((peers,)),
            dma((peers,)),
            dma((peers,)),
            dma((8,)),
            dma((8,)),
        ],
        compiler_params=pltpu.CompilerParams(
            collective_id=0, has_side_effects=True, vmem_limit_bytes=50 * 1024 * 1024
        ),
    )(
        grid_latent,
        mesh_latent.reshape(nodes, ch),
        block_owner,
        block_sender,
        block_receiver,
        block_feature,
        mesh_sender,
        mesh_receiver,
        mesh_feature,
        *weights,
    )
    return out.reshape(rows_lat, rows_lon, ch)


def solution(mesh):
    band = P(("lon", "lat", "sub"), None)
    band3 = P(("lon", "lat", "sub"), None, None)
    place = P(("groups", "lat"), ("lon", "sub"), None)
    in_specs = (
        P(("groups", "lon", "lat", "sub"), None),
        place,
        band,
        band,
        band,
        band3,
        band,
        band,
        band3,
    ) + (P(),) * 18
    return jax.shard_map(
        on_device, mesh=mesh, in_specs=in_specs, out_specs=place, check_vma=False
    )
```

time: 117 us -> 65.7 us (0.56)
  Pallas kernels: 0 us -> 44.3 us
  waiting for transfers between devices: 30.7 us -> 0 us
  starting transfers between devices: 23.4 us -> 0 us
  matrix products: 22.6 us -> 0 us
  other arithmetic: 12 us -> 0 us
  local copies, waits for them, and re-layouts: 26.4 us -> 20.5 us
    pallas_call x0 -> x1, Pallas kernels: none -> 44.3 us  [on_device(): pl.pallas_call(functools.partial(kernel, peers, subs, lats), out_shape=ja...]
    all_to_all x3 -> x0, waiting for transfers between devices: 26.9 us -> none  [the longest x1 22.4 us: on_device(): lax.all_to_all(outgoing.reshape(peer_count, CAP, block_rows, channels), (...]
    dot_general x18 -> x0, matrix products: 22.6 us -> none  [the longest x2 5.2 us: node_update(): jnp.dot(summed.astype(jnp.bfloat16), input_weight[channels:], preferred_e...]
    gather x6 -> x0, local copies, waits for them, and re-layouts: 22 us -> none  [the longest x1 9.91 us: on_device(): send_rows = lookup[mesh_sender.reshape(-1)]]
    unnamed x44 -> x56, local copies, waits for them, and re-layouts: 0.36 us -> 20.5 us
    all_to_all x3 -> x0, starting transfers between devices: 15 us -> none  [the longest x1 6.33 us: on_device(): lax.all_to_all(targets.reshape(peer_count, CAP, block_rows), ('lon', 'sub...]
    ppermute x4 -> x0, starting transfers between devices: 8.41 us -> none  [the longest x2 5.01 us: with_halo(): after = lax.ppermute(first, axis, down)]
    ppermute x4 -> x0, waiting for transfers between devices: 3.73 us -> none  [the longest x2 3.73 us: with_halo(): after = lax.ppermute(first, axis, down)]
  transfers between devices with their start and end apart: 7 -> 0, of which waited for: 3 -> 0; matrix products, arithmetic and copies ran while one was open for 20% -> 0% of each run, Pallas kernels for 0% -> 0%
where the time goes in v1:
time: 65.7 us; the launch traced here: 64.9 us
  Pallas kernels  44.3 us (67%)
  local copies, waits for them, and re-layouts  20.5 us (31%)
    pallas_call x1, Pallas kernels, on_device(): pl.pallas_call(functools.partial(kernel, peers, subs, lats), out_shape=ja...  44.3 us
    unnamed x56, local copies, waits for them, and re-layouts  20.5 us

profile of v1, /device:TPU:0, one launch (start us, length us, event | category | flops | bytes accessed | tf_op | source)
XLA Modules:
  0.0 64.9 jit_solution(5156839491359787209)
XLA Ops:
  0.0 0.0 copy-start.10
  0.0 0.0 copy-start.26
  0.0 0.7 %copy-done.26 = s32[8,1]{0,1:T(1,128)S(1)} copy-done((s32[8,1]{0,1:T(1,128)S(1)}, s32[8,1]{0,1:T(1,128)}, u32[]{:S(2)}) %copy-start.26) | copy-done | bytes 56
  0.7 0.0 copy-start.18
  0.7 0.1 copy.28.owner_ref
  0.8 0.0 copy-done.10
  0.8 0.0 copy-done.14
  0.8 0.6 copy-done.18
  1.4 0.0 copy-start
  1.4 1.0 %copy-done = bf16[1024,256]{1,0:T(8,128)(2,1)S(1)} copy-done((bf16[1024,256]{1,0:T(8,128)(2,1)S(1)}, bf16[1024,256]{1,0:T(8,128)(2,1)}, u32[]{:S(2)}) %copy-start) | copy-done | bytes 524312
  2.4 1.0 %copy-done.1 = f32[8,64,256]{2,1,0:T(8,128)S(1)} copy-done((f32[8,64,256]{2,1,0:T(8,128)S(1)}, f32[8,64,256]{2,1,0:T(8,128)}, u32[]{:S(2)}) %copy-start.1) | copy-done | bytes 524312
  3.4 0.0 copy-start.2
  3.4 0.9 %copy-done.2 = bf16[512,256]{1,0:T(8,128)(2,1)S(1)} copy-done((bf16[512,256]{1,0:T(8,128)(2,1)S(1)}, bf16[512,256]{1,0:T(8,128)(2,1)}, u32[]{:S(2)}) %copy-start.2) | copy-done | bytes 262168
  4.4 0.0 copy-start.3
  4.4 0.9 %copy-done.3 = bf16[512,256]{1,0:T(8,128)(2,1)S(1)} copy-done((bf16[512,256]{1,0:T(8,128)(2,1)S(1)}, bf16[512,256]{1,0:T(8,128)(2,1)}, u32[]{:S(2)}) %copy-start.3) | copy-done | bytes 262168
  5.3 0.0 copy-start.4
  5.3 0.9 %copy-done.4 = bf16[512,256]{1,0:T(8,128)(2,1)S(1)} copy-done((bf16[512,256]{1,0:T(8,128)(2,1)S(1)}, bf16[512,256]{1,0:T(8,128)(2,1)}, u32[]{:S(2)}) %copy-start.4) | copy-done | bytes 262168
  6.3 0.0 copy-start.5
  6.3 0.9 %copy-done.5 = bf16[512,256]{1,0:T(8,128)(2,1)S(1)} copy-done((bf16[512,256]{1,0:T(8,128)(2,1)S(1)}, bf16[512,256]{1,0:T(8,128)(2,1)}, u32[]{:S(2)}) %copy-start.5) | copy-done | bytes 262168
  7.2 0.0 copy-start.6
  7.2 0.9 %copy-done.6 = bf16[256,256]{1,0:T(8,128)(2,1)S(1)} copy-done((bf16[256,256]{1,0:T(8,128)(2,1)S(1)}, bf16[256,256]{1,0:T(8,128)(2,1)}, u32[]{:S(2)}) %copy-start.6) | copy-done | bytes 131096
  8.1 0.0 copy-start.7
  8.1 0.9 %copy-done.7 = bf16[256,256]{1,0:T(8,128)(2,1)S(1)} copy-done((bf16[256,256]{1,0:T(8,128)(2,1)S(1)}, bf16[256,256]{1,0:T(8,128)(2,1)}, u32[]{:S(2)}) %copy-start.7) | copy-done | bytes 131096
  9.0 0.0 copy-start.8
  9.1 0.9 %copy-done.8 = bf16[256,256]{1,0:T(8,128)(2,1)S(1)} copy-done((bf16[256,256]{1,0:T(8,128)(2,1)S(1)}, bf16[256,256]{1,0:T(8,128)(2,1)}, u32[]{:S(2)}) %copy-start.8) | copy-done | bytes 131096
  10.0 0.0 copy-start.9
  10.0 0.9 %copy-done.9 = bf16[256,256]{1,0:T(8,128)(2,1)S(1)} copy-done((bf16[256,256]{1,0:T(8,128)(2,1)S(1)}, bf16[256,256]{1,0:T(8,128)(2,1)}, u32[]{:S(2)}) %copy-start.9) | copy-done | bytes 131096
  10.9 0.0 copy-start.11
  10.9 0.7 %copy-done.11 = bf16[8,4,128]{2,1,0:T(4,128)(2,1)S(1)} copy-done((bf16[8,4,128]{2,1,0:T(4,128)(2,1)S(1)}, bf16[8,4,128]{2,1,0:T(4,128)(2,1)}, u32[]{:S(2)}) %copy-start.11) | copy-done | bytes 8216
  11.6 0.0 copy-start.12
  11.6 0.7 %copy-done.12 = s32[16,128]{1,0:T(8,128)S(1)} copy-done((s32[16,128]{1,0:T(8,128)S(1)}, s32[16,128]{1,0:T(8,128)}, u32[]{:S(2)}) %copy-start.12) | copy-done | bytes 8216
  12.3 0.0 copy-start.13
  12.3 0.7 %copy-done.13 = s32[16,128]{1,0:T(8,128)S(1)} copy-done((s32[16,128]{1,0:T(8,128)S(1)}, s32[16,128]{1,0:T(8,128)}, u32[]{:S(2)}) %copy-start.13) | copy-done | bytes 8216
  12.9 0.0 copy-start.15
  13.0 0.7 %copy-done.15 = s32[8,128]{1,0:T(8,128)S(1)} copy-done((s32[8,128]{1,0:T(8,128)S(1)}, s32[8,128]{1,0:T(8,128)}, u32[]{:S(2)}) %copy-start.15) | copy-done | bytes 4120
  13.6 0.0 copy-start.16
  13.6 0.7 %copy-done.16 = f32[4,256]{1,0:T(4,128)S(1)} copy-done((f32[4,256]{1,0:T(4,128)S(1)}, f32[4,256]{1,0:T(4,128)}, u32[]{:S(2)}) %copy-start.16) | copy-done | bytes 4120
  14.3 0.7 %copy-done.17 = f32[4,256]{1,0:T(4,128)S(1)} copy-done((f32[4,256]{1,0:T(4,128)S(1)}, f32[4,256]{1,0:T(4,128)}, u32[]{:S(2)}) %copy-start.17) | copy-done | bytes 4120
  15.0 0.0 copy-start.19
  15.0 0.7 %copy-done.19 = f32[256]{0:T(256)S(1)} copy-done((f32[256]{0:T(256)S(1)}, f32[256]{0:T(256)}, u32[]{:S(2)}) %copy-start.19) | copy-done | bytes 1048
  15.7 0.7 %copy-done.20 = f32[256]{0:T(256)S(1)} copy-done((f32[256]{0:T(256)S(1)}, f32[256]{0:T(256)}, u32[]{:S(2)}) %copy-start.20) | copy-done | bytes 1048
  16.4 0.7 %copy-done.21 = f32[256]{0:T(256)S(1)} copy-done((f32[256]{0:T(256)S(1)}, f32[256]{0:T(256)}, u32[]{:S(2)}) %copy-start.21) | copy-done | bytes 1048
  17.1 0.7 %copy-done.22 = f32[256]{0:T(256)S(1)} copy-done((f32[256]{0:T(256)S(1)}, f32[256]{0:T(256)}, u32[]{:S(2)}) %copy-start.22) | copy-done | bytes 1048
  17.7 0.7 %copy-done.23 = f32[256]{0:T(256)S(1)} copy-done((f32[256]{0:T(256)S(1)}, f32[256]{0:T(256)}, u32[]{:S(2)}) %copy-start.23) | copy-done | bytes 1048
  18.4 0.7 %copy-done.24 = f32[256]{0:T(256)S(1)} copy-done((f32[256]{0:T(256)S(1)}, f32[256]{0:T(256)}, u32[]{:S(2)}) %copy-start.24) | copy-done | bytes 1048
  19.1 0.7 %copy-done.25 = f32[256]{0:T(256)S(1)} copy-done((f32[256]{0:T(256)S(1)}, f32[256]{0:T(256)}, u32[]{:S(2)}) %copy-start.25) | copy-done | bytes 1048
  19.8 44.3 %shard_map.253 = f32[512,256]{1,0:T(8,128)S(1)} custom-call(bf16[1024,256]{1,0:T(8,128)(2,1)S(1)} %copy-done, f32[512,256]{1,0:T(8,128)S(1)} %bitcast.11, s32[8,1]{1,0:T(8,128)S(1)} %copy.28.owner_ref, s32[8,128]{1,0:T(8,128)S(1)} %copy-done.14, s32[8,128]{1,0:T(8,128)S(1)} %copy-done.15, bf16[8,4,128]{2,1,0:T(4,128)(2,1)S(1)} %copy-done.11, ...), custom_call_target="tpu_custom_call" | custom-call | tf_op jit(solution)/shard_map/pallas_call | solution.py:400
  64.1 0.8 %copy.30 = f32[8,64,256]{2,1,0:T(8,128)} copy(f32[8,64,256]{2,1,0:T(8,128)S(1)} %bitcast.10) | data formatting | bytes 1048576
  (9 shorter events, 0.0 us)
Async XLA Ops:
  0.0 0.8 %copy-start.10 = (bf16[16,4,128]{2,1,0:T(4,128)(2,1)S(1)}, bf16[16,4,128]{2,1,0:T(4,128)(2,1)}, u32[]{:S(2)}) copy-start(bf16[16,4,128]{2,1,0:T(4,128)(2,1)} %mfeat_ref.1) | copy-start | bytes 49156
  0.0 0.7 %copy-start.26 = (s32[8,1]{0,1:T(1,128)S(1)}, s32[8,1]{0,1:T(1,128)}, u32[]{:S(2)}) copy-start(s32[8,1]{0,1:T(1,128)} %param.29) | copy-start | bytes 100
  0.0 0.8 %copy-start.14 = (s32[8,128]{1,0:T(8,128)S(1)}, s32[8,128]{1,0:T(8,128)}, u32[]{:S(2)}) copy-start(s32[8,128]{1,0:T(8,128)} %bsend_ref.1) | copy-start | bytes 12292
  0.7 0.7 %copy-start.18 = (f32[256]{0:T(256)S(1)}, f32[256]{0:T(256)}, u32[]{:S(2)}) copy-start(f32[256]{0:T(256)} %param.38) | copy-start | bytes 3076
  1.4 1.0 %copy-start = (bf16[1024,256]{1,0:T(8,128)(2,1)S(1)}, bf16[1024,256]{1,0:T(8,128)(2,1)}, u32[]{:S(2)}) copy-start(bf16[1024,256]{1,0:T(8,128)(2,1)} %grid_ref.1) | copy-start | bytes 1572868
  2.4 1.0 %copy-start.1 = (f32[8,64,256]{2,1,0:T(8,128)S(1)}, f32[8,64,256]{2,1,0:T(8,128)}, u32[]{:S(2)}) copy-start(f32[8,64,256]{2,1,0:T(8,128)} %param.28) | copy-start | bytes 1572868
  3.4 0.9 %copy-start.2 = (bf16[512,256]{1,0:T(8,128)(2,1)S(1)}, bf16[512,256]{1,0:T(8,128)(2,1)}, u32[]{:S(2)}) copy-start(bf16[512,256]{1,0:T(8,128)(2,1)} %eei.1) | copy-start | bytes 786436
  4.4 0.9 %copy-start.3 = (bf16[512,256]{1,0:T(8,128)(2,1)S(1)}, bf16[512,256]{1,0:T(8,128)(2,1)}, u32[]{:S(2)}) copy-start(bf16[512,256]{1,0:T(8,128)(2,1)} %eni.1) | copy-start | bytes 786436
  5.3 0.9 %copy-start.4 = (bf16[512,256]{1,0:T(8,128)(2,1)S(1)}, bf16[512,256]{1,0:T(8,128)(2,1)}, u32[]{:S(2)}) copy-start(bf16[512,256]{1,0:T(8,128)(2,1)} %pei.1) | copy-start | bytes 786436
  6.3 0.9 %copy-start.5 = (bf16[512,256]{1,0:T(8,128)(2,1)S(1)}, bf16[512,256]{1,0:T(8,128)(2,1)}, u32[]{:S(2)}) copy-start(bf16[512,256]{1,0:T(8,128)(2,1)} %pni.1) | copy-start | bytes 786436
  7.2 0.9 %copy-start.6 = (bf16[256,256]{1,0:T(8,128)(2,1)S(1)}, bf16[256,256]{1,0:T(8,128)(2,1)}, u32[]{:S(2)}) copy-start(bf16[256,256]{1,0:T(8,128)(2,1)} %eeo.1) | copy-start | bytes 393220
  8.1 0.9 %copy-start.7 = (bf16[256,256]{1,0:T(8,128)(2,1)S(1)}, bf16[256,256]{1,0:T(8,128)(2,1)}, u32[]{:S(2)}) copy-start(bf16[256,256]{1,0:T(8,128)(2,1)} %eno.1) | copy-start | bytes 393220
  9.0 0.9 %copy-start.8 = (bf16[256,256]{1,0:T(8,128)(2,1)S(1)}, bf16[256,256]{1,0:T(8,128)(2,1)}, u32[]{:S(2)}) copy-start(bf16[256,256]{1,0:T(8,128)(2,1)} %peo.1) | copy-start | bytes 393220
  10.0 0.9 %copy-start.9 = (bf16[256,256]{1,0:T(8,128)(2,1)S(1)}, bf16[256,256]{1,0:T(8,128)(2,1)}, u32[]{:S(2)}) copy-start(bf16[256,256]{1,0:T(8,128)(2,1)} %pno.1) | copy-start | bytes 393220
  10.9 0.7 %copy-start.11 = (bf16[8,4,128]{2,1,0:T(4,128)(2,1)S(1)}, bf16[8,4,128]{2,1,0:T(4,128)(2,1)}, u32[]{:S(2)}) copy-start(bf16[8,4,128]{2,1,0:T(4,128)(2,1)} %bfeat_ref.1) | copy-start | bytes 24580
  11.6 0.7 %copy-start.12 = (s32[16,128]{1,0:T(8,128)S(1)}, s32[16,128]{1,0:T(8,128)}, u32[]{:S(2)}) copy-start(s32[16,128]{1,0:T(8,128)} %msend_ref.1) | copy-start | bytes 24580
  12.3 0.7 %copy-start.13 = (s32[16,128]{1,0:T(8,128)S(1)}, s32[16,128]{1,0:T(8,128)}, u32[]{:S(2)}) copy-start(s32[16,128]{1,0:T(8,128)} %mrecv_ref.1) | copy-start | bytes 24580
  12.9 0.7 %copy-start.15 = (s32[8,128]{1,0:T(8,128)S(1)}, s32[8,128]{1,0:T(8,128)}, u32[]{:S(2)}) copy-start(s32[8,128]{1,0:T(8,128)} %brecv_ref.1) | copy-start | bytes 12292
  13.6 0.7 %copy-start.16 = (f32[4,256]{1,0:T(4,128)S(1)}, f32[4,256]{1,0:T(4,128)}, u32[]{:S(2)}) copy-start(f32[4,256]{1,0:T(4,128)} %eef.1) | copy-start | bytes 12292
  14.3 0.7 %copy-start.17 = (f32[4,256]{1,0:T(4,128)S(1)}, f32[4,256]{1,0:T(4,128)}, u32[]{:S(2)}) copy-start(f32[4,256]{1,0:T(4,128)} %pef.1) | copy-start | bytes 12292
  15.0 0.7 %copy-start.19 = (f32[256]{0:T(256)S(1)}, f32[256]{0:T(256)}, u32[]{:S(2)}) copy-start(f32[256]{0:T(256)} %param.40) | copy-start | bytes 3076
  15.7 0.7 %copy-start.20 = (f32[256]{0:T(256)S(1)}, f32[256]{0:T(256)}, u32[]{:S(2)}) copy-start(f32[256]{0:T(256)} %param.42) | copy-start | bytes 3076
  16.4 0.7 %copy-start.21 = (f32[256]{0:T(256)S(1)}, f32[256]{0:T(256)}, u32[]{:S(2)}) copy-start(f32[256]{0:T(256)} %param.44) | copy-start | bytes 3076
  17.1 0.7 %copy-start.22 = (f32[256]{0:T(256)S(1)}, f32[256]{0:T(256)}, u32[]{:S(2)}) copy-start(f32[256]{0:T(256)} %param.47) | copy-start | bytes 3076
  17.7 0.7 %copy-start.23 = (f32[256]{0:T(256)S(1)}, f32[256]{0:T(256)}, u32[]{:S(2)}) copy-start(f32[256]{0:T(256)} %param.49) | copy-start | bytes 3076
  18.4 0.7 %copy-start.24 = (f32[256]{0:T(256)S(1)}, f32[256]{0:T(256)}, u32[]{:S(2)}) copy-start(f32[256]{0:T(256)} %param.51) | copy-start | bytes 3076
  19.1 0.7 %copy-start.25 = (f32[256]{0:T(256)S(1)}, f32[256]{0:T(256)}, u32[]{:S(2)}) copy-start(f32[256]{0:T(256)} %param.53) | copy-start | bytes 3076

commit v2 on v1

--- a/solution.py
+++ b/solution.py
@@ -33,14 +33,6 @@
     return jnp.where(match, 1.0, 0.0).astype(BF)
 
 
-def split3(w):
-    a = w.astype(BF)
-    r = w - a.astype(F32)
-    b = r.astype(BF)
-    c = (r - b.astype(F32)).astype(BF)
-    return a, b, c
-
-
 def feature_term(feat_t, w_ref):
     total = feat_t[:, 0:1] * w_ref[0:1, :]
     for f in range(1, w_ref.shape[0]):
@@ -52,57 +44,74 @@
     peers,
     subs,
     lats,
-    grid_ref,
-    mesh_ref,
-    owner_ref,
-    bsend_ref,
-    brecv_ref,
-    bfeat_ref,
-    msend_ref,
-    mrecv_ref,
-    mfeat_ref,
-    eei,
-    eef,
-    eeb,
-    eeo,
-    eeg,
-    eni,
-    enb,
-    eno,
-    eng,
-    pei,
-    pef,
-    peb,
-    peo,
-    peg,
-    pni,
-    pnb,
-    pno,
-    png,
-    out_ref,
-    gproj,
-    blkpre,
-    send,
-    meta_s,
-    recv,
-    meta_r,
-    acc,
-    ptab,
-    table,
-    packs,
-    halo_rows,
-    halo_packs,
-    menc,
-    oh,
-    oht,
-    fbase,
-    send_sem,
-    recv_sem,
-    msend_sem,
-    mrecv_sem,
-    hsend_sem,
-    hrecv_sem,
+    *refs,
 ):
+    inputs, rest = refs[:27], refs[27:]
+    (
+        out_ref,
+        gproj,
+        blkpre,
+        send,
+        meta_s,
+        recv,
+        meta_r,
+        acc,
+        ptab,
+        table,
+        packs,
+        halo_rows,
+        halo_packs,
+        menc,
+        oh,
+        oht,
+        fbase,
+        pedges,
+        send_sem,
+        recv_sem,
+        msend_sem,
+        mrecv_sem,
+        hsend_sem,
+        hrecv_sem,
+        in_sem,
+    ) = rest[:25]
+    staged = rest[25:]
+    loads = [
+        pltpu.make_async_copy(src, dst, in_sem.at[n])
+        for n, (src, dst) in enumerate(zip(inputs, staged))
+    ]
+    early = [3, 0, 9, 5, 10, 11, 2, 4]
+    late = [n for n in range(27) if n not in early]
+    for n in early + late:
+        loads[n].start()
+    (
+        grid_ref,
+        mesh_ref,
+        owner_ref,
+        bsend_ref,
+        brecv_ref,
+        bfeat_ref,
+        msend_ref,
+        mrecv_ref,
+        mfeat_ref,
+        eei,
+        eef,
+        eeb,
+        eeo,
+        eeg,
+        eni,
+        enb,
+        eno,
+        eng,
+        pei,
+        pef,
+        peb,
+        peo,
+        peg,
+        pni,
+        pnb,
+        pno,
+        png,
+    ) = staged
     grid_rows, ch = grid_ref.shape
     nodes = mesh_ref.shape[0]
     blocks, eb = bsend_ref.shape
@@ -138,6 +147,8 @@
                     barrier, inc=1, device_id=at(me + dp, lat + dl), device_id_type=MESH
                 )
 
+    for n in early:
+        loads[n].wait()
     gproj[...] = dot(grid_ref[...], eei[:ch, :]).astype(BF)
     send_t = bsend_ref[...].astype(F32).T.astype(jnp.int32)
     lane_g = lax.broadcasted_iota(jnp.int32, (eb, grid_rows), 1)
@@ -158,7 +169,7 @@
         s0 = jnp.int32(0)
         s1 = jnp.int32(0)
         for b in range(blocks):
-            m = owner_ref[b, 0] == q
+            m = owner_ref[0, b] == q
             s0 = jnp.where(m & (n == 0), b, s0)
             s1 = jnp.where(m & (n == 1), b, s1)
             n = n + m.astype(jnp.int32)
@@ -200,6 +211,8 @@
     lax.fori_loop(0, peers - 1, send_step, 0)
     fill(0)
 
+    for n in late:
+        loads[n].wait()
     mesh_bf = mesh_ref[...].astype(BF)
     ptab[...] = dot(mesh_bf, eei[ch:, :]).astype(BF)
     acc[...] = jnp.zeros_like(acc)
@@ -214,15 +227,18 @@
     row_id = jnp.where(above, a + rows + W, jnp.where(below, a + W, a))
     local = jnp.where(above, a + rows, jnp.where(below, a - rows, a))
     which = jnp.where(above, 0, jnp.where(below, 2, 1))
-    base = nodes + 2 * W * 64
+    edge = W * 64
+    halo = 2 * nodes
+    base = halo + 2 * edge
     left = b_ < 0
     inner = (~left) & (b_ < 64)
     side = jnp.where(left, 0, 3)
     bb = jnp.where(left, b_ + W, b_ - 64)
-    cell = jnp.where(inner, row_id * 64 + b_, base + (side + which) * 16 + local * W + bb)
+    inside_id = row_id * 64 + b_ + jnp.where(row_id < rows, 0, nodes)
+    cell = jnp.where(inner, inside_id, base + (side + which) * 16 + local * W + bb)
     cell_t = cell.astype(F32).T.astype(jnp.int32)
     mrecv = mrecv_ref[...]
-    recv_base = base + 96
+    recv_base = nodes
     mrecv_t = (mrecv + recv_base).astype(F32).T.astype(jnp.int32)
     width = table.shape[0]
     lane_t = lax.broadcasted_iota(jnp.int32, (eb, width), 1)
@@ -280,8 +296,6 @@
     packs[0] = packed[0:16]
     packs[1] = packed[16:32]
 
-    edge = W * 64
-
     def side_copy(dp, dl):
         n = (0 if dp == 1 else 3) + (1 - dl)
         return pltpu.make_async_remote_copy(
@@ -319,7 +333,12 @@
     side_copy(1, 0).start()
     side_copy(-1, 0).start()
     table[recv_base : recv_base + nodes, :] = dot(enc_bf, pei[ch:, :]).astype(BF)
-    table[recv_base + nodes :, :] = jnp.zeros((width - recv_base - nodes, ch), BF)
+    table[base + 96 :, :] = jnp.zeros((width - base - 96, ch), BF)
+    step = 4 * eb
+    chunks = pblocks * eb // step
+    for i in range(chunks):
+        part = pl.ds(i * step, step)
+        fbase[part, :] += dot(oh[part, :halo], table[:halo, :])
     own_in = dot(enc_bf, pni[:ch, :]) + pnb[...]
 
     for dl in (-1, 1):
@@ -331,13 +350,13 @@
             band_copy(-dl).wait_recv()
             side_copy(1, -dl).wait_recv()
             side_copy(-1, -dl).wait_recv()
-            table[pl.ds(nodes + n * edge, edge), :] = halo_rows[n]
+            table[pl.ds(halo + n * edge, edge), :] = halo_rows[n]
             for m in slots:
                 table[pl.ds(base + m * 16, 16), :] = halo_packs[m]
 
         @pl.when(jnp.logical_not(inside(dl)))
         def _():
-            table[pl.ds(nodes + n * edge, edge), :] = jnp.zeros((edge, ch), BF)
+            table[pl.ds(halo + n * edge, edge), :] = jnp.zeros((edge, ch), BF)
             for m in slots:
                 table[pl.ds(base + m * 16, 16), :] = jnp.zeros((16, ch), BF)
 
@@ -346,19 +365,13 @@
     table[pl.ds(base + 16, 16), :] = halo_packs[1]
     table[pl.ds(base + 64, 16), :] = halo_packs[4]
 
-    acc[...] = jnp.zeros_like(acc)
-    step = 4 * eb
-
-    def process(i, carry):
-        first = pl.multiple_of(i * step, step)
-        pre = dot(oh[pl.ds(first, step), :], table[...]) + fbase[pl.ds(first, step), :]
-        hidden = silu(pre).astype(BF)
-        edges = layer_norm(dot(hidden, peo[...]), peg[...]).astype(BF)
-        acc[...] += dot(oht[:, pl.ds(first, step)], edges)
-        return carry
-
-    lax.fori_loop(0, pblocks * eb // step, process, 0)
-    pre = own_in + dot(acc[...].astype(BF), pni[ch:, :])
+    for i in range(chunks):
+        part = pl.ds(i * step, step)
+        pre = fbase[part, :] + dot(oh[part, halo:], table[halo:, :])
+        projected = dot(silu(pre).astype(BF), peo[...])
+        pedges[part, :] = layer_norm(projected, peg[...]).astype(BF)
+    summed = dot(oht[...], pedges[...])
+    pre = own_in + dot(summed.astype(BF), pni[ch:, :])
     out_ref[...] = menc[...] + layer_norm(dot(silu(pre).astype(BF), pno[...]), png[...])
 
     for dl in (-1, 1):
@@ -394,14 +407,27 @@
     pblocks = mesh_sender.shape[0]
     weights = [w.reshape(1, -1) if w.ndim == 1 else w for w in weights]
     width = 1408
-    vm = pl.BlockSpec(memory_space=pltpu.VMEM)
-    sm = pl.BlockSpec(memory_space=pltpu.SMEM)
+    inputs = [
+        grid_latent,
+        mesh_latent.reshape(nodes, ch),
+        block_owner.reshape(1, blocks),
+        block_sender,
+        block_receiver,
+        block_feature,
+        mesh_sender,
+        mesh_receiver,
+        mesh_feature,
+        *weights,
+    ]
+    staged = [
+        (pltpu.SMEM if n == 2 else pltpu.VMEM)(x.shape, x.dtype) for n, x in enumerate(inputs)
+    ]
     dma = pltpu.SemaphoreType.DMA
     out = pl.pallas_call(
         functools.partial(kernel, peers, subs, lats),
         out_shape=jax.ShapeDtypeStruct((nodes, ch), F32),
-        in_specs=[vm, vm, sm] + [vm] * (6 + len(weights)),
-        out_specs=vm,
+        in_specs=[pl.BlockSpec(memory_space=pl.ANY)] * len(inputs),
+        out_specs=pl.BlockSpec(memory_space=pltpu.VMEM),
         scratch_shapes=[
             pltpu.VMEM(grid_latent.shape, BF),
             pltpu.VMEM((blocks, eb, ch), BF),
@@ -419,28 +445,20 @@
             pltpu.VMEM((pblocks * eb, width), BF),
             pltpu.VMEM((nodes, pblocks * eb), BF),
             pltpu.VMEM((pblocks * eb, ch), F32),
+            pltpu.VMEM((pblocks * eb, ch), BF),
             dma((peers,)),
             dma((peers,)),
             dma((peers,)),
             dma((peers,)),
             dma((8,)),
             dma((8,)),
-        ],
+            dma((len(inputs),)),
+        ]
+        + staged,
         compiler_params=pltpu.CompilerParams(
-            collective_id=0, has_side_effects=True, vmem_limit_bytes=50 * 1024 * 1024
+            collective_id=0, has_side_effects=True, vmem_limit_bytes=64 * 1024 * 1024
         ),
-    )(
-        grid_latent,
-        mesh_latent.reshape(nodes, ch),
-        block_owner,
-        block_sender,
-        block_receiver,
-        block_feature,
-        mesh_sender,
-        mesh_receiver,
-        mesh_feature,
-        *weights,
-    )
+    )(*inputs)
     return out.reshape(rows_lat, rows_lon, ch)
 
 

time: 65.7 us -> 44 us (0.67)
  local copies, waits for them, and re-layouts: 20.5 us -> 1.87 us
  Pallas kernels: 44.3 us -> 41.9 us
    unnamed x56 -> x1, local copies, waits for them, and re-layouts: 20.5 us -> 1.87 us
    pallas_call x1, Pallas kernels: 44.3 us -> 41.9 us  [on_device(): pl.pallas_call(functools.partial(kernel, peers, subs, lats), out_shape=ja...]
where the time goes in v2:
time: 44 us; the launch traced here: 43.8 us
  Pallas kernels  41.9 us (95%)
  local copies, waits for them, and re-layouts  1.87 us (4%)
    pallas_call x1, Pallas kernels, on_device(): pl.pallas_call(functools.partial(kernel, peers, subs, lats), out_shape=ja...  41.9 us
    unnamed x1, local copies, waits for them, and re-layouts  1.87 us

profile of v2, /device:TPU:0, one launch (start us, length us, event | category | flops | bytes accessed | tf_op | source)
XLA Modules:
  0.0 43.8 jit_solution(9031166023069781275)
XLA Ops:
  0.0 41.9 %shard_map.253 = f32[512,256]{1,0:T(8,128)} custom-call(bf16[1024,256]{1,0:T(8,128)(2,1)} %refs_0_.1, f32[512,256]{1,0:T(8,128)} %bitcast.12, s32[1,8]{1,0:T(1,128)} %bitcast.21, s32[8,128]{1,0:T(8,128)} %refs_3_.1, s32[8,128]{1,0:T(8,128)} %refs_4_.1, bf16[8,4,128]{2,1,0:T(4,128)(2,1)} %refs_5_.1, s32[16,128]{1,0:T(8,128)} %refs_6_.1, s32[16,128]{1,0:T(8,128)} %refs_7_.1, ...), custom_call_target="tpu_custom_call" | custom-call | tf_op jit(solution)/shard_map/pallas_call | solution.py:426
  42.0 1.9 %copy.29 = f32[8,64,256]{2,1,0:T(8,128)} copy(f32[8,64,256]{2,1,0:T(8,128)} %bitcast.11) | data formatting | bytes 1048576

commit v3 on v2

--- a/solution.py
+++ b/solution.py
@@ -66,6 +66,8 @@
         oht,
         fbase,
         pedges,
+        picks,
+        spread,
         send_sem,
         recv_sem,
         msend_sem,
@@ -73,8 +75,8 @@
         hsend_sem,
         hrecv_sem,
         in_sem,
-    ) = rest[:25]
-    staged = rest[25:]
+    ) = rest[:27]
+    staged = rest[27:]
     loads = [
         pltpu.make_async_copy(src, dst, in_sem.at[n])
         for n, (src, dst) in enumerate(zip(inputs, staged))
@@ -122,7 +124,6 @@
     lat = lax.axis_index("lat")
     sub = lax.axis_index("sub")
     me = lon * subs + sub
-    half = peers // 2
 
     def at(p, l=None):
         p = lax.rem(p + 2 * peers, peers)
@@ -161,7 +162,7 @@
     pl.semaphore_wait(barrier, peers - 1 + 3 * bands)
 
     def offset(i):
-        return jnp.where(lax.rem(i, 2) == 0, half + i // 2, half - (i + 1) // 2)
+        return jnp.where(lax.rem(i, 2) == 0, 1 + i // 2, peers - 1 - i // 2)
 
     def fill(k):
         q = lax.rem(me + k, peers)
@@ -203,12 +204,15 @@
     def send_step(i, carry):
         k = offset(i)
         fill(k)
-        data, meta = copies(k)
-        meta.start()
-        data.start()
+        copies(k)[1].start()
         return carry
 
+    def data_step(i, carry):
+        copies(offset(i))[0].start()
+        return carry
+
     lax.fori_loop(0, peers - 1, send_step, 0)
+    lax.fori_loop(0, peers - 1, data_step, 0)
     fill(0)
 
     for n in late:
@@ -252,29 +256,35 @@
 
     lane_n = lax.broadcasted_iota(jnp.int32, (eb, nodes), 1)
 
-    def encode(data, meta):
+    def prepare(k, meta):
         ids = meta[...]
         ids_t = ids.astype(F32).T.astype(jnp.int32)
-        parts = []
         for j in range(CAP):
-            picked = dot(one_hot(ids_t[:, j : j + 1] == lane_n), ptab[...])
-            pre = picked + data[pl.ds(j * eb, eb), :].astype(F32)
-            parts.append(silu(pre).astype(BF))
-        hidden = jnp.concatenate(parts, axis=0)
+            part = pl.ds(j * eb, eb)
+            picks[k, part, :] = dot(one_hot(ids_t[:, j : j + 1] == lane_n), ptab[...])
+            spread[k, :, part] = one_hot(sub_n == ids[j : j + 1, :])
+
+    def encode(k, data):
+        pre = picks[k] + data[...].astype(F32)
+        hidden = silu(pre).astype(BF)
         edges = layer_norm(dot(hidden, eeo[...]), eeg[...]).astype(BF)
-        spread = jnp.concatenate(
-            [one_hot(sub_n == ids[j : j + 1, :]) for j in range(CAP)], axis=1
-        )
-        acc[...] += dot(spread, edges)
-
-    encode(send.at[0], meta_s.at[0])
+        acc[...] += dot(spread[k], edges)
+
+    prepare(0, meta_s.at[0])
+    encode(0, send.at[0])
+
+    def meta_step(i, carry):
+        k = offset(i)
+        copies(k)[1].wait()
+        prepare(k, meta_r.at[k])
+        return carry
+
+    lax.fori_loop(0, peers - 1, meta_step, 0)
 
     def recv_step(i, carry):
         k = offset(i)
-        data, meta = copies(k)
-        meta.wait()
-        data.wait()
-        encode(recv.at[k], meta_r.at[k])
+        copies(k)[0].wait()
+        encode(k, recv.at[k])
         return carry
 
     lax.fori_loop(0, peers - 1, recv_step, 0)
@@ -446,6 +456,8 @@
             pltpu.VMEM((nodes, pblocks * eb), BF),
             pltpu.VMEM((pblocks * eb, ch), F32),
             pltpu.VMEM((pblocks * eb, ch), BF),
+            pltpu.VMEM((peers, CAP * eb, ch), F32),
+            pltpu.VMEM((peers, nodes, CAP * eb), BF),
             dma((peers,)),
             dma((peers,)),
             dma((peers,)),

time: 44 us -> 43.1 us (0.980)
  Pallas kernels: 41.9 us -> 41.1 us
    pallas_call x1, Pallas kernels: 41.9 us -> 41.1 us  [on_device(): pl.pallas_call(functools.partial(kernel, peers, subs, lats), out_shape=ja...]
where the time goes in v3:
time: 43.1 us; the launch traced here: 42.9 us
  Pallas kernels  41.1 us (95%)
  local copies, waits for them, and re-layouts  1.87 us (4%)
    pallas_call x1, Pallas kernels, on_device(): pl.pallas_call(functools.partial(kernel, peers, subs, lats), out_shape=ja...  41.1 us
    unnamed x1, local copies, waits for them, and re-layouts  1.87 us

profile of v3, /device:TPU:0, one launch (start us, length us, event | category | flops | bytes accessed | tf_op | source)
XLA Modules:
  0.0 42.9 jit_solution(7004411570868977186)
XLA Ops:
  0.0 41.1 %shard_map.253 = f32[512,256]{1,0:T(8,128)} custom-call(bf16[1024,256]{1,0:T(8,128)(2,1)} %refs_0_.1, f32[512,256]{1,0:T(8,128)} %bitcast.12, s32[1,8]{1,0:T(1,128)} %bitcast.21, s32[8,128]{1,0:T(8,128)} %refs_3_.1, s32[8,128]{1,0:T(8,128)} %refs_4_.1, bf16[8,4,128]{2,1,0:T(4,128)(2,1)} %refs_5_.1, s32[16,128]{1,0:T(8,128)} %refs_6_.1, s32[16,128]{1,0:T(8,128)} %refs_7_.1, ...), custom_call_target="tpu_custom_call" | custom-call | tf_op jit(solution)/shard_map/pallas_call | solution.py:436
  41.1 1.9 %copy.29 = f32[8,64,256]{2,1,0:T(8,128)} copy(f32[8,64,256]{2,1,0:T(8,128)} %bitcast.11) | data formatting | bytes 1048576
